TPU v7x, 32 devices: a whole 2x2x4 slice. The times are simulated.
32 devices in a mesh: groups: 2 (over x), dom: 16 (over z, y, core).
Axes of the slice: x: 2, y: 2, z: 4, core: 2. Of those that a mesh axis runs over, the one named last changes fastest.
Arguments:
- adjoint_start: float32 [6, 128, 64, 128], P(None, None, ('groups', 'dom')), parts along dimension 2, may hold values from -6 to 6
- source: float32 [6, 128, 64, 128], P(None, None, ('groups', 'dom')), parts along dimension 2, may hold values from -6 to 6
- state: bfloat16 [6, 128, 64, 128], P(None, None, ('groups', 'dom')), parts along dimension 2, may hold values from -0.4 to 4, as said below
- pseudo_step: float32 [128, 64, 128], P(None, ('groups', 'dom')), parts along dimension 1, may hold values from 0.04 to 0.16
- row_counts: int32 [12], P('groups'), parts along dimension 0, may hold values from 1 to 8, as said below
Outputs:
- adjoint: float32 [6, 128, 64, 128], P(None, None, ('groups', 'dom')), parts along dimension 2
There are 2 independent parts, one for each index of `groups`. A program takes and returns all parts, laid end to end along the dimension named above; each array names one. Nothing has to cross between parts.
Inputs may be any that keep to these rules, and one draw needn't show every extreme that they name: `state`: component 0 (density) lies in 0.7 to 1.3, components 1 to 3 (momenta) in -0.4 to 0.4, component 5 in 0.5 to 2, and the pressure 0.4 (e - 0.5 |m|^2 / density) of every cell in 0.6 to 1.4. `row_counts`: the counts sum to 16; every row holds at least 1 block, and one row holds exactly 8.
All inputs are finite; a program needn't handle non-finite values.
Results may differ from a plain program's by a relative error of at most 0.0003.
Values may be sent and summed in bfloat16 or wider, within the bound.
A program may use at most 64 MiB of HBM per device.

v0:
```python
import jax
import jax.numpy as jnp
from jax import lax
from jax.sharding import PartitionSpec as P

BANDS = 256
ROWS = 6
ITERS = 2


damping = 2.0


def padded(block, sides, width):
    for axis, dim in sides:
        count = lax.axis_size(axis)
        forward = [(i, i + 1) for i in range(count - 1)]
        backward = [(target, source) for source, target in forward]
        low = lax.ppermute(
            lax.slice_in_dim(block, block.shape[dim] - width, None, axis=dim), axis, forward
        )
        high = lax.ppermute(lax.slice_in_dim(block, 0, width, axis=dim), axis, backward)
        block = jnp.concatenate([low, block, high], axis=dim)
    return block


def fluxes(flow):
    density = flow[0]
    momentum = flow[1:4]
    energy = flow[4]
    viscous = flow[5]
    velocity = momentum / density
    pressure = 0.4 * (energy - 0.5 * jnp.sum(momentum * velocity, axis=0))
    result = []
    for direction in range(3):
        parts = [momentum[direction]]
        for other in range(3):
            term = momentum[other] * velocity[direction]
            if other == direction:
                term = term + pressure
            parts.append(term)
        parts.append(velocity[direction] * (energy + pressure))
        parts.append(velocity[direction] * viscous)
        result.append(jnp.stack(parts))
    return tuple(result)


def transposed(centre, below_side, above_side, inlet_ghost, outlet_ghost, flow):
    pitch_minus = jnp.roll(centre, 1, axis=1)
    pitch_plus = jnp.roll(centre, -1, axis=1)
    axial_minus = jnp.concatenate([inlet_ghost, centre[..., :-1]], axis=3)
    axial_plus = jnp.concatenate([centre[..., 1:], outlet_ghost], axis=3)
    cotangent = (
        0.5 * (pitch_minus - pitch_plus),
        0.5 * (below_side - above_side),
        0.5 * (axial_minus - axial_plus),
    )
    unused, pullback = jax.vjp(fluxes, flow)
    convected = pullback(cotangent)[0]
    spread = (
        6.0 * centre - pitch_minus - pitch_plus - below_side - above_side - axial_minus - axial_plus
    )
    return convected + 0.5 * damping * spread


def intersection(position, row_cells):
    band_ids = jnp.arange(BANDS, dtype=jnp.int32)[None, :]
    low_end = jnp.maximum(position[:, None] * BANDS, band_ids * row_cells)
    high_end = jnp.minimum((position[:, None] + 1) * BANDS, (band_ids + 1) * row_cells)
    return jnp.maximum(high_end - low_end, 0).astype(jnp.float32)


def on_device(adjoint_start, source, state, pseudo_step, row_counts):
    comps_count = adjoint_start.shape[0]
    pitch_cells = adjoint_start.shape[1]
    rad_cells = adjoint_start.shape[2]
    highest = lax.Precision.HIGHEST
    device = lax.axis_index("dom")
    row_ends = jnp.cumsum(row_counts)
    row_starts = row_ends - row_counts
    my_row = jnp.sum((device >= row_ends).astype(jnp.int32))
    first_cell = row_starts[my_row] * rad_cells
    row_cells = row_counts[my_row] * rad_cells
    row_ids = jnp.arange(ROWS, dtype=jnp.int32)
    own_select = (row_ids == my_row).astype(jnp.float32)
    prev_select = (row_ids == my_row - 1).astype(jnp.float32)
    next_select = (row_ids == my_row + 1).astype(jnp.float32)

    def positions(cell_count):
        return device * rad_cells + jnp.arange(cell_count, dtype=jnp.int32) - first_cell

    inner_weights = intersection(positions(rad_cells), row_cells)
    inner_scaled = inner_weights / (pitch_cells * row_cells).astype(jnp.float32)
    adjoint = adjoint_start
    for sweep_index in range(ITERS):
        sums_in = jnp.sum(adjoint[..., 0], axis=1)
        sums_out = jnp.sum(adjoint[..., -1], axis=1)
        part_in = jnp.dot(sums_in, inner_scaled, precision=highest)
        part_out = jnp.dot(sums_out, inner_scaled, precision=highest)
        stacked = jnp.stack([part_in, part_out])
        contribution = own_select[:, None, None, None] * stacked[None]
        table = lax.psum(contribution, "dom")
        extended = padded(adjoint, (("dom", 2),), 1)
        position = positions(rad_cells)
        weights = intersection(position, row_cells)
        in_row = ((position >= 0) & (position < row_cells))[None, None, :, None]
        below_ok = (position >= 1)[None, None, :, None]
        above_ok = (position + 1 < row_cells)[None, None, :, None]
        centre = extended[:, :, 1:-1]
        below_side = jnp.where(below_ok, extended[:, :, :-2], 0.0)
        above_side = jnp.where(above_ok, extended[:, :, 2:], 0.0)
        prof_prev = jnp.tensordot(prev_select, table[:, 1], axes=1, precision=highest)
        prof_next = jnp.tensordot(next_select, table[:, 0], axes=1, precision=highest)
        inlet_vals = jnp.dot(prof_prev, weights.T, precision=highest) / BANDS
        outlet_vals = jnp.dot(prof_next, weights.T, precision=highest) / BANDS
        inlet_ghost = jnp.broadcast_to(
            inlet_vals[:, None, :, None], (comps_count, pitch_cells, rad_cells, 1)
        )
        outlet_ghost = jnp.broadcast_to(
            outlet_vals[:, None, :, None], (comps_count, pitch_cells, rad_cells, 1)
        )
        flow = jnp.where(in_row, state.astype(jnp.float32), 1.0)
        image = transposed(centre, below_side, above_side, inlet_ghost, outlet_ghost, flow)
        adjoint = centre - pseudo_step[None] * (image - source)
    return adjoint


def solution(mesh):
    return jax.shard_map(
        on_device,
        mesh=mesh,
        in_specs=(
            P(None, None, ("groups", "dom"), None),
            P(None, None, ("groups", "dom"), None),
            P(None, None, ("groups", "dom"), None),
            P(None, ("groups", "dom"), None),
            P("groups"),
        ),
        out_specs=P(None, None, ("groups", "dom"), None),
        check_vma=False,
    )
```

profile of v0, /device:TPU:0, one launch (start us, length us, event | category | flops | bytes accessed | tf_op | source)
XLA Modules:
  0.0 242.4 jit_solution(2166825126034697752)
XLA Ops:
  13.9 2.5 %slice_reduce_fusion.3 = (f32[6,2]{1,0:T(8,128)S(1)}, f32[6,2]{1,0:T(8,128)S(1)}) fusion(f32[6,128,2,128]{3,2,1,0:T(2,128)} %param.5), kind=kLoop, calls=%fused_computation.35 | loop fusion | flops 3048 | bytes 12384 | tf_op jit(solution)/shard_map/reduce_sum | solution.py:96
  18.2 0.9 fusion.55
  19.1 2.4 collective-permute-start
  21.5 1.3 collective-permute-start.1
  22.8 1.2 fusion.54
  24.8 1.1 subtract_multiply_fusion.3
  27.3 1.6 copy.10
  28.9 79.2 %all-reduce.63.cloned.1.call-done = f32[6,2,6,256]{3,2,1,0:T(8,128)} async-done(((f32[6,2,6,256]{3,2,1,0:T(8,128)}), f32[6,2,6,256]{3,2,1,0:T(8,128)}) %all-reduce.63.cloned.1.call-update) | async-done | bytes 73744 | tf_op jit(solution)/shard_map/psum | solution.py:102
  112.8 1.2 subtract_multiply_fusion.4
  114.3 1.0 copy-done.8
  118.2 1.8 multiply_subtract_fusion.1
  120.1 0.9 fusion.51
  121.4 1.4 fusion.50
  123.0 2.0 collective-permute-start.2
  125.0 1.3 collective-permute-start.3
  129.0 1.0 slice_multiply_fusion.18
  130.0 87.4 %all-reduce.65.cloned.1.call-done = f32[6,2,6,256]{3,2,1,0:T(8,128)} async-done(((f32[6,2,6,256]{3,2,1,0:T(8,128)}), f32[6,2,6,256]{3,2,1,0:T(8,128)}) %all-reduce.65.cloned.1.call-update) | async-done | bytes 73744 | tf_op jit(solution)/shard_map/psum | solution.py:102
  219.9 1.3 copy.27
  221.2 1.4 convolution_multiply_fusion
  222.6 1.3 copy.28
  226.2 1.3 subtract_multiply_fusion.1
  227.7 1.0 copy-done.10
  232.1 1.9 multiply_subtract_fusion
  234.0 1.5 copy.30
  (179 shorter events, 24.8 us)
Async XLA Ops:
  6.5 101.6 %all-reduce.63.cloned.1.call-start = ((), (), s32[]{:S(2)}) async-start(), calls=%async_computation | async-start | bytes 196608 | tf_op jit(solution)/shard_map/psum | solution.py:102
  9.5 7.8 %copy-start.47 = (f32[6]{0:T(128)}, f32[6]{0:T(128)S(1)}, u32[]{:S(2)}) copy-start(f32[6]{0:T(128)S(1)} %compare_convert_fusion) | copy-start | bytes 76
  12.7 3.8 %copy-start.50 = (s32[2]{0:T(128)}, s32[2]{0:T(128)S(1)}, u32[]{:S(2)}) copy-start(s32[2]{0:T(128)S(1)} %get-tuple-element.19) | copy-start | bytes 28
  12.7 3.7 %copy-start.54 = (s32[2]{0:T(128)}, s32[2]{0:T(128)S(1)}, u32[]{:S(2)}) copy-start(s32[2]{0:T(128)S(1)} %broadcast_multiply_fusion.2) | copy-start | bytes 28
  13.3 3.2 %copy-start.39 = (s32[256]{0:T(256)}, s32[256]{0:T(256)S(1)}, u32[]{:S(2)}) copy-start(s32[256]{0:T(256)S(1)} %get-tuple-element.126) | copy-start | bytes 3076
  13.3 3.2 %copy-start.42 = (s32[256]{0:T(256)}, s32[256]{0:T(256)S(1)}, u32[]{:S(2)}) copy-start(s32[256]{0:T(256)S(1)} %get-tuple-element.127) | copy-start | bytes 3076
  13.9 4.2 %copy-start = (f32[6,128,2,128]{3,2,1,0:T(2,128)S(1)}, f32[6,128,2,128]{3,2,1,0:T(2,128)}, u32[]{:S(2)}) copy-start(f32[6,128,2,128]{3,2,1,0:T(2,128)} %param.5) | copy-start | bytes 2359300
  18.1 199.3 %all-reduce.65.cloned.1.call-start = ((), (), s32[]{:S(2)}) async-start(), calls=%async_computation.1 | async-start | bytes 196608 | tf_op jit(solution)/shard_map/psum | solution.py:102
  19.1 92.9 %collective-permute-start = (f32[6,128,1,128]{3,1,2,0:T(8,128)}, f32[6,128,1,128]{3,1,2,0:T(8,128)S(1)}, u32[]{:S(2)}, u32[]{:S(2)}) collective-permute-start(f32[6,128,1,128]{3,1,2,0:T(8,128)} %get-tuple-element.106), channel_id=1, source_target_pairs={{0,1},{1,2},{2,3},{3,4},{4,5},{5,6},{6,7},{7,8},{8,9},{9,10},{10,1... | collective-permute-start | bytes 1179656 | tf_op jit(solution)/shard_map/ppermute | solution.py:19
  21.5 90.5 %collective-permute-start.1 = (f32[6,128,1,128]{3,1,2,0:T(8,128)}, f32[6,128,1,128]{3,1,2,0:T(8,128)}, u32[]{:S(2)}, u32[]{:S(2)}) collective-permute-start(f32[6,128,1,128]{3,1,2,0:T(8,128)} %get-tuple-element.105), channel_id=1, source_target_pairs={{1,0},{2,1},{3,2},{4,3},{5,4},{6,5},{7,6},{8,7},{9,8},{10,9},{11,1... | collective-permute-start | bytes 1179656 | tf_op jit(solution)/shard_map/ppermute | solution.py:22
  24.0 86.6 %copy-start.5 = (f32[6,128,2,127]{3,1,2,0:T(8,128)}, f32[6,128,2,127]{3,1,2,0:T(8,128)S(1)}, u32[]{:S(2)}) copy-start(f32[6,128,2,127]{3,1,2,0:T(8,128)S(1)} %get-tuple-element.103) | copy-start | bytes 2340868
  112.0 2.0 copy-start.18
  114.1 1.7 copy-start.16
  114.3 1.3 copy-start.11
  116.4 1.4 copy-start.14
  116.8 1.3 copy-start.2
  116.8 1.4 copy-start.19
  116.9 1.4 copy-start.20
  123.0 3.3 %copy-start.34 = (f32[2,256]{1,0:T(2,128)S(1)}, f32[2,256]{1,0:T(2,128)}, u32[]{:S(2)}) copy-start(f32[2,256]{1,0:T(2,128)} %copy-done.33) | copy-start | bytes 6148
  123.0 103.1 %collective-permute-start.2 = (f32[6,128,1,128]{3,1,2,0:T(8,128)}, f32[6,128,1,128]{3,1,2,0:T(8,128)}, u32[]{:S(2)}, u32[]{:S(2)}) collective-permute-start(f32[6,128,1,128]{3,1,2,0:T(8,128)} %get-tuple-element.84), channel_id=1, source_target_pairs={{0,1},{1,2},{2,3},{3,4},{4,5},{5,6},{6,7},{7,8},{8,9},{9,10},{10,1... | collective-permute-start | bytes 1179656 | tf_op jit(solution)/shard_map/ppermute | solution.py:19
  125.0 101.1 %collective-permute-start.3 = (f32[6,128,1,128]{3,1,2,0:T(8,128)}, f32[6,128,1,128]{3,1,2,0:T(8,128)}, u32[]{:S(2)}, u32[]{:S(2)}) collective-permute-start(f32[6,128,1,128]{3,1,2,0:T(8,128)} %get-tuple-element.83), channel_id=1, source_target_pairs={{1,0},{2,1},{3,2},{4,3},{5,4},{6,5},{7,6},{8,7},{9,8},{10,9},{11,1... | collective-permute-start | bytes 1179656 | tf_op jit(solution)/shard_map/ppermute | solution.py:22
  223.8 1.7 copy-start.3
  223.9 1.7 copy-start.4
  226.1 1.4 copy-start.13
  (39 other events, 35.4 us)
Sparse Core Ops, SparseCore 0:
  18.2 89.8 all-reduce.62
  128.1 89.2 all-reduce.64
where the time goes:
time: 243 us; the launch traced here: 242 us
  waiting for transfers between devices  167 us (69%)
  local copies, waits for them, and re-layouts  27 us (11%)
  between operations  19.5 us (8%)
  other arithmetic  18 us (7%)
  starting transfers between devices  7.03 us (3%)
  matrix products  4.25 us (2%)
    psum x2, waiting for transfers between devices, on_device(): table = lax.psum(contribution, 'dom')  167 us
    unnamed x116, local copies, waits for them, and re-layouts  13.2 us
  transfers between devices with their start and end apart: 6, of which 2 were waited for; matrix products, arithmetic and copies ran while one was open for 8% of the time, Pallas kernels for 0%

commit v1 on v0

v1 whole, which is shorter than its diff:
```python
import functools

import jax
import jax.numpy as jnp
from jax import lax
from jax.experimental import pallas as pl
from jax.experimental.pallas import tpu as pltpu
from jax.sharding import PartitionSpec as P

BANDS = 256
ROWS = 6
SWEEPS = 2
LANES = 128
PAD = 8
GROUP = 16
MESH = pl.DeviceIdType.MESH
HALO = jnp.float32


def total(parts):
    result = parts[0]
    for part in parts[1:]:
        result = result + part
    return result


def update(c, pm, pp, lo, hi, am, ap, prim, source, step):
    v, enthalpy, ratio, kinetic = prim[:3], prim[3], prim[4], prim[5]
    comps = range(len(c))
    a = [
        [pm[i] - pp[i] for i in comps],
        [lo[i] - hi[i] for i in comps],
        [am[i] - ap[i] for i in comps],
    ]
    by_velocity = [
        total([a[d][1 + k] * v[k] for k in range(3)]) + a[d][4] * enthalpy + a[d][5] * ratio
        for d in range(3)
    ]
    energy = total([a[d][4] * v[d] for d in range(3)])
    by_pressure = a[0][1] + a[1][2] + a[2][3] + energy
    scaled = 0.4 * by_pressure
    convected = [kinetic * by_pressure - total([v[d] * by_velocity[d] for d in range(3)])]
    for k in range(3):
        convected.append(
            a[k][0]
            + total([a[d][1 + k] * v[d] for d in range(3)])
            - v[k] * scaled
            + by_velocity[k]
        )
    convected.append(energy + scaled)
    convected.append(total([a[d][5] * v[d] for d in range(3)]))
    result = []
    for i in comps:
        around = (pm[i] + pp[i]) + (lo[i] + hi[i]) + (am[i] + ap[i])
        image = 0.5 * convected[i] + (6.0 * c[i] - around)
        result.append(c[i] - step * (image - source[i]))
    return result


def kernel(
    n, comps, pitch, chunks,
    counts, adj_in, src_in, st_in, ps_in, out,
    adj, src, st, ps, prim, mid, fin,
    snd_dn, snd_up, rcv_lo, rcv_hi, gsend, gath, ghost, weight,
    load_sem, store_sem, dn_send, dn_recv, up_send, up_recv, g_send, g_recv,
):
    cells = 2 * pitch
    span = pitch // chunks
    me = lax.axis_index("dom")
    f32 = jnp.float32

    loads = [
        pltpu.make_async_copy(adj_in, adj.at[:, pl.ds(PAD, cells), :], load_sem.at[0]),
        pltpu.make_async_copy(st_in, st, load_sem.at[1]),
        pltpu.make_async_copy(src_in, src, load_sem.at[2]),
        pltpu.make_async_copy(ps_in, ps, load_sem.at[3]),
    ]
    for load in loads:
        load.start()

    barrier = pltpu.get_barrier_semaphore()
    for k in range(1, n):
        pl.semaphore_signal(
            barrier, inc=1, device_id={"dom": lax.rem(me + k, n)}, device_id_type=MESH
        )

    lane = lax.broadcasted_iota(jnp.int32, (1, LANES), 1)

    starts, ends = [], []
    end = jnp.int32(0)
    for r in range(ROWS):
        starts.append(end)
        end = end + counts[r]
        ends.append(end)

    def placed(dev):
        row = total([(dev >= e).astype(jnp.int32) for e in ends])
        start = jnp.zeros_like(row)
        count = jnp.zeros_like(row)
        for r in range(ROWS):
            start = jnp.where(row == r, starts[r], start)
            count = jnp.where(row == r, counts[r], count)
        return row, start, count

    band = lax.broadcasted_iota(jnp.int32, (1, BANDS), 1)

    def overlap(position, row_cells):
        low = jnp.maximum(position * BANDS, band * row_cells)
        high = jnp.minimum((position + 1) * BANDS, (band + 1) * row_cells)
        return jnp.maximum(high - low, 0).astype(f32)

    mine = jnp.full((1, 1), me, jnp.int32)
    my_row, my_start, my_count = placed(mine)
    dev = me - lax.broadcasted_iota(jnp.int32, (n, 1), 0)
    dev = jnp.where(dev < 0, dev + n, dev)
    row, start, count = placed(dev)
    from_next = (row == my_row + 1).astype(f32)
    from_prev = (row == my_row - 1).astype(f32)
    own = [overlap(2 * (mine - my_start) + i, 2 * my_count) for i in range(2)]
    theirs = [overlap(2 * (dev - start) + r, 2 * count) for r in range(2)]
    scale = 1.0 / (pitch * BANDS * 2 * count).astype(f32)
    for i in range(2):
        dots = [jnp.sum(theirs[r] * own[i], axis=1, keepdims=True) * scale for r in range(2)]
        weight[i] = jnp.where(
            lane < 8, from_next * dots[0],
            jnp.where(
                lane < 16, from_next * dots[1],
                jnp.where(
                    lane < 24, from_prev * dots[0],
                    jnp.where(lane < 32, from_prev * dots[1], 0.0),
                ),
            ),
        )

    place = jnp.zeros((1, LANES), jnp.int32) + (mine - my_start)
    below_ok = place > 0
    above_ok = place + 1 < my_count

    def send_sums(sweep, sums):
        message = jnp.zeros((1, LANES), f32)
        for r in range(2):
            for c in range(comps):
                whole = jnp.sum(sums[r][c], axis=0, keepdims=True)
                at = c + 8 * r
                message = jnp.where(lane == at, pltpu.roll(whole, at, 1) if at else whole, message)
                message = jnp.where(lane == at + 16, pltpu.roll(whole, at + 17, 1), message)
        gsend[sweep] = message
        gath[sweep, 0] = message

    def sums_copy(sweep, k):
        return pltpu.make_async_remote_copy(
            src_ref=gsend.at[sweep],
            dst_ref=gath.at[sweep, k],
            send_sem=g_send.at[sweep, k],
            recv_sem=g_recv.at[sweep, k],
            device_id={"dom": lax.rem(me + k, n)},
            device_id_type=MESH,
        )

    def down_copy(sweep, ch):
        return pltpu.make_async_remote_copy(
            src_ref=snd_dn.at[sweep, ch],
            dst_ref=rcv_hi.at[sweep, ch],
            send_sem=dn_send.at[sweep, ch],
            recv_sem=dn_recv.at[sweep, ch],
            device_id={"dom": jnp.maximum(me - 1, 0)},
            device_id_type=MESH,
        )

    def up_copy(sweep, ch):
        return pltpu.make_async_remote_copy(
            src_ref=snd_up.at[sweep, ch],
            dst_ref=rcv_lo.at[sweep, ch],
            send_sem=up_send.at[sweep, ch],
            recv_sem=up_recv.at[sweep, ch],
            device_id={"dom": jnp.minimum(me + 1, n - 1)},
            device_id_type=MESH,
        )

    def send_halo(sweep, ch):
        @pl.when(me > 0)
        def _():
            down_copy(sweep, ch).start()

        @pl.when(me < n - 1)
        def _():
            up_copy(sweep, ch).start()

    def wrap(field):
        field[:, PAD - 2 : PAD, :] = field[:, PAD + cells - 2 : PAD + cells, :]
        field[:, PAD + cells : PAD + cells + 2, :] = field[:, PAD : PAD + 2, :]

    zero_sums = tuple(jnp.zeros((8, LANES), f32) for _ in range(2 * comps))

    def added(sums, r, values):
        sums = list(sums)
        for c in range(comps):
            for part in range(GROUP // 8):
                sums[r * comps + c] = sums[r * comps + c] + values[c][8 * part : 8 * part + 8]
        return tuple(sums)

    def split(sums):
        return [sums[:comps], sums[comps:]]

    loads[0].wait()

    def first(ch, sums):
        for part in range(span // GROUP):
            at = pl.multiple_of(PAD + 2 * (ch * span + part * GROUP), 8)
            for r in range(2):
                values = [
                    adj[c, pl.ds(at + r, GROUP, stride=2), :] for c in range(comps)
                ]
                target = (snd_dn, snd_up)[r]
                for c in range(comps):
                    target[0, ch, c, part * GROUP : (part + 1) * GROUP, :] = values[c].astype(HALO)
                sums = added(sums, r, values)
        return sums

    sums = lax.fori_loop(0, chunks, first, zero_sums)
    send_sums(0, split(sums))
    pl.semaphore_wait(barrier, n - 1)
    for k in range(1, n):
        sums_copy(0, k).start()

    def send_first(ch, carry):
        send_halo(0, ch)
        return carry

    lax.fori_loop(0, chunks, send_first, 0)
    wrap(adj)

    loads[1].wait()

    def primitive(j, carry):
        at = pl.ds(pl.multiple_of(j * 16, 16), 16)
        flow = [st[c, at, :].astype(f32) for c in range(6)]
        inverse = 1.0 / flow[0]
        v = [flow[1 + d] * inverse for d in range(3)]
        kinetic = 0.5 * total([flow[1 + d] * v[d] for d in range(3)])
        pressure = 0.4 * (flow[4] - kinetic)
        values = v + [(flow[4] + pressure) * inverse, flow[5] * inverse, 0.4 * kinetic * inverse]
        for c in range(6):
            prim[c, at, :] = values[c]
        return carry

    lax.fori_loop(0, cells // 16, primitive, 0)
    loads[2].wait()
    loads[3].wait()

    for sweep in range(SWEEPS):
        last = sweep == SWEEPS - 1
        old = adj if sweep == 0 else mid
        for k in range(1, n):
            sums_copy(sweep, k).wait_recv()
        gathered = gath[sweep][:, 0, :]
        for i in range(2):
            mixed = jnp.sum(weight[i] * gathered, axis=0, keepdims=True)
            mixed = mixed + pltpu.roll(mixed, LANES - 8, 1)
            for c in range(comps):
                ghost[sweep, i, c] = jnp.where(
                    lane == 0,
                    pltpu.roll(mixed, LANES - 16 - c, 1),
                    pltpu.roll(mixed, LANES - 1 - c, 1),
                )

        def advance(ch, sums, sweep=sweep, last=last, old=old):
            @pl.when(me < n - 1)
            def _():
                down_copy(sweep, ch).wait_recv()

            @pl.when(me > 0)
            def _():
                up_copy(sweep, ch).wait_recv()

            for part in range(span // GROUP):
                at = pl.multiple_of(2 * (ch * span + part * GROUP), 2 * GROUP)
                piece = slice(part * GROUP, (part + 1) * GROUP)
                for r in range(2):
                    def near(offset):
                        return [
                            old[c, pl.ds(PAD + at + r + offset, GROUP, stride=2), :]
                            for c in range(comps)
                        ]

                    def here(ref, c):
                        return ref[c, pl.ds(at + r, GROUP, stride=2), :]

                    centre, before, after = near(0), near(-2), near(2)
                    if r == 0:
                        below = [
                            jnp.where(below_ok, rcv_lo[sweep, ch, c, piece, :].astype(f32), 0.0)
                            for c in range(comps)
                        ]
                        above = near(1)
                    else:
                        below = near(-1)
                        above = [
                            jnp.where(above_ok, rcv_hi[sweep, ch, c, piece, :].astype(f32), 0.0)
                            for c in range(comps)
                        ]
                    fore = [
                        jnp.where(lane == 0, ghost[sweep, r, c], pltpu.roll(centre[c], 1, 1))
                        for c in range(comps)
                    ]
                    aft = [
                        jnp.where(
                            lane == LANES - 1, ghost[sweep, r, c],
                            pltpu.roll(centre[c], LANES - 1, 1),
                        )
                        for c in range(comps)
                    ]
                    values = update(
                        centre, before, after, below, above, fore, aft,
                        [here(prim, c) for c in range(6)],
                        [here(src, c) for c in range(comps)],
                        ps[pl.ds(at + r, GROUP, stride=2), :],
                    )
                    for c in range(comps):
                        if last:
                            fin[c, pl.ds(at + r, GROUP, stride=2), :] = values[c]
                        else:
                            mid[c, pl.ds(PAD + at + r, GROUP, stride=2), :] = values[c]
                            target = (snd_dn, snd_up)[r]
                            target[sweep + 1, ch, c, piece, :] = values[c].astype(HALO)
                    if not last:
                        sums = added(sums, r, values)
            if last:
                store(ch).start()
            else:
                send_halo(sweep + 1, ch)
            return sums

        def store(ch):
            at = pl.ds(pl.multiple_of(2 * span * ch, 2 * span), 2 * span)
            return pltpu.make_async_copy(fin.at[:, at, :], out.at[:, at, :], store_sem.at[ch])

        sums = lax.fori_loop(0, chunks, advance, () if last else zero_sums)
        if not last:
            send_sums(sweep + 1, split(sums))
            for k in range(1, n):
                sums_copy(sweep + 1, k).start()
            wrap(mid)

    def finish(ch, carry):
        for sweep in range(SWEEPS):
            @pl.when(me > 0)
            def _():
                down_copy(sweep, ch).wait_send()

            @pl.when(me < n - 1)
            def _():
                up_copy(sweep, ch).wait_send()
        store(ch).wait()
        return carry

    lax.fori_loop(0, chunks, finish, 0)
    for sweep in range(SWEEPS):
        for k in range(1, n):
            sums_copy(sweep, k).wait_send()


def on_device(n, chunks, adjoint_start, source, state, pseudo_step, row_counts):
    comps, pitch, rad, lanes = adjoint_start.shape
    cells = pitch * rad
    span = pitch // chunks
    flat = (comps, cells, lanes)
    f32 = jnp.float32
    hbm = pl.BlockSpec(memory_space=pl.ANY)
    dma = pltpu.SemaphoreType.DMA
    padded = (comps, cells + 2 * PAD, lanes)
    halo = (SWEEPS, chunks, comps, span, lanes)
    result = pl.pallas_call(
        functools.partial(kernel, n, comps, pitch, chunks),
        out_shape=jax.ShapeDtypeStruct(flat, f32),
        in_specs=[pl.BlockSpec(memory_space=pltpu.SMEM), hbm, hbm, hbm, hbm],
        out_specs=hbm,
        scratch_shapes=[
            pltpu.VMEM(padded, f32),
            pltpu.VMEM(flat, f32),
            pltpu.VMEM(flat, jnp.bfloat16),
            pltpu.VMEM((cells, lanes), f32),
            pltpu.VMEM((6, cells, lanes), f32),
            pltpu.VMEM(padded, f32),
            pltpu.VMEM(flat, f32),
            pltpu.VMEM(halo, HALO),
            pltpu.VMEM(halo, HALO),
            pltpu.VMEM(halo, HALO),
            pltpu.VMEM(halo, HALO),
            pltpu.VMEM((SWEEPS, 1, lanes), f32),
            pltpu.VMEM((SWEEPS, n, 1, lanes), f32),
            pltpu.VMEM((SWEEPS, 2, comps, 1, lanes), f32),
            pltpu.VMEM((2, n, lanes), f32),
            dma((4,)),
            dma((chunks,)),
            dma((SWEEPS, chunks)),
            dma((SWEEPS, chunks)),
            dma((SWEEPS, chunks)),
            dma((SWEEPS, chunks)),
            dma((SWEEPS, n)),
            dma((SWEEPS, n)),
        ],
        compiler_params=pltpu.CompilerParams(
            collective_id=0, has_side_effects=True, vmem_limit_bytes=32 * 1024 * 1024
        ),
    )(
        row_counts,
        adjoint_start.reshape(flat),
        source.reshape(flat),
        state.reshape(flat),
        pseudo_step.reshape(cells, lanes),
    )
    return result.reshape(adjoint_start.shape)


def solution(mesh):
    return jax.shard_map(
        functools.partial(on_device, mesh.shape["dom"], 8),
        mesh=mesh,
        in_specs=(
            P(None, None, ("groups", "dom"), None),
            P(None, None, ("groups", "dom"), None),
            P(None, None, ("groups", "dom"), None),
            P(None, ("groups", "dom"), None),
            P("groups"),
        ),
        out_specs=P(None, None, ("groups", "dom"), None),
        check_vma=False,
    )
```

time: 243 us -> 34 us (0.14)
  waiting for transfers between devices: 167 us -> 0 us
  Pallas kernels: 0 us -> 28 us
  local copies, waits for them, and re-layouts: 27 us -> 5.7 us
  between operations: 19.5 us -> 0.01 us
  other arithmetic: 18 us -> 0 us
  starting transfers between devices: 7.03 us -> 0 us
  matrix products: 4.25 us -> 0 us
    psum x2 -> x0, waiting for transfers between devices: 167 us -> none  [on_device(): table = lax.psum(contribution, 'dom')]
    pallas_call x0 -> x1, Pallas kernels: none -> 28 us  [on_device(): pl.pallas_call(functools.partial(kernel, n, comps, pitch, chunks), out_sh...]
    mul x19 -> x0, other arithmetic: 7.76 us -> none  [the longest x2 2.52 us: transposed(): 0.5 * (below_side - above_side)]
    unnamed x116 -> x11, local copies, waits for them, and re-layouts: 13.2 us -> 5.7 us
    ppermute x4 -> x0, starting transfers between devices: 6.99 us -> none  [the longest x2 4.42 us: padded(): lax.ppermute(lax.slice_in_dim(block, block.shape[dim] - width, None, axis...]
    slice x8 -> x0, local copies, waits for them, and re-layouts: 4.8 us -> none  [the longest x2 2.62 us: transposed(): axial_minus = jnp.concatenate([inlet_ghost, centre[..., :-1]], axis=3)]
    dot_general x12 -> x0, matrix products: 4.25 us -> none  [the longest x2 1.62 us: on_device(): outlet_vals = jnp.dot(prof_next, weights.T, precision=highest) / BANDS]
    sub x2 -> x0, other arithmetic: 3.79 us -> none  [on_device(): adjoint = centre - pseudo_step[None] * (image - source)]
  transfers between devices with their start and end apart: 6 -> 0, of which waited for: 2 -> 0; matrix products, arithmetic and copies ran while one was open for 8% -> 0% of each run, Pallas kernels for 0% -> 0%
where the time goes in v1:
time: 34 us; the launch traced here: 33.7 us
  Pallas kernels  28 us (82%)
  local copies, waits for them, and re-layouts  5.7 us (17%)
    pallas_call x1, Pallas kernels, on_device(): pl.pallas_call(functools.partial(kernel, n, comps, pitch, chunks), out_sh...  28 us
    unnamed x11, local copies, waits for them, and re-layouts  5.7 us

profile of v1, /device:TPU:0, one launch (start us, length us, event | category | flops | bytes accessed | tf_op | source)
XLA Modules:
  0.0 33.7 jit_solution(1870652206386232123)
XLA Ops:
  0.0 0.0 copy-start.4
  0.0 0.7 %copy-done.4 = s32[6]{0:T(128)S(1)} copy-done((s32[6]{0:T(128)S(1)}, s32[6]{0:T(128)}, u32[]{:S(2)}) %copy-start.4) | copy-done | bytes 48
  0.7 0.0 copy-start
  0.7 1.1 %copy-done = f32[6,128,2,128]{3,2,1,0:T(2,128)S(1)} copy-done((f32[6,128,2,128]{3,2,1,0:T(2,128)S(1)}, f32[6,128,2,128]{3,2,1,0:T(2,128)}, u32[]{:S(2)}) %copy-start) | copy-done | bytes 786456
  1.8 0.0 copy-start.1
  1.8 1.1 %copy-done.1 = f32[6,128,2,128]{3,2,1,0:T(2,128)S(1)} copy-done((f32[6,128,2,128]{3,2,1,0:T(2,128)S(1)}, f32[6,128,2,128]{3,2,1,0:T(2,128)}, u32[]{:S(2)}) %copy-start.1) | copy-done | bytes 786456
  2.9 0.0 copy-start.2
  2.9 1.0 %copy-done.2 = bf16[6,128,2,128]{3,2,1,0:T(2,128)(2,1)S(1)} copy-done((bf16[6,128,2,128]{3,2,1,0:T(2,128)(2,1)S(1)}, bf16[6,128,2,128]{3,2,1,0:T(2,128)(2,1)}, u32[]{:S(2)}) %copy-start.2) | copy-done | bytes 393240
  3.9 0.0 copy-start.3
  3.9 0.9 %copy-done.3 = f32[128,2,128]{2,1,0:T(2,128)S(1)} copy-done((f32[128,2,128]{2,1,0:T(2,128)S(1)}, f32[128,2,128]{2,1,0:T(2,128)}, u32[]{:S(2)}) %copy-start.3) | copy-done | bytes 131096
  4.8 28.0 %shard_map.55 = f32[6,256,128]{2,1,0:T(8,128)S(1)} custom-call(s32[6]{0:T(128)S(1)} %copy-done.4, f32[6,256,128]{2,1,0:T(8,128)S(1)} %bitcast.6, f32[6,256,128]{2,1,0:T(8,128)S(1)} %bitcast.7, bf16[6,256,128]{2,1,0:T(8,128)(2,1)S(1)} %bitcast.8, f32[256,128]{1,0:T(8,128)S(1)} %bitcast.9), custom_call_target="tpu_custom_call" | custom-call | tf_op jit(solution)/shard_map/pallas_call | solution.py:373
  32.8 0.9 %copy.7 = f32[6,128,2,128]{3,2,1,0:T(2,128)} copy(f32[6,128,2,128]{3,2,1,0:T(2,128)S(1)} %bitcast.5) | data formatting | bytes 1572864
Async XLA Ops:
  0.0 0.7 %copy-start.4 = (s32[6]{0:T(128)S(1)}, s32[6]{0:T(128)}, u32[]{:S(2)}) copy-start(s32[6]{0:T(128)} %counts.1) | copy-start | bytes 76
  0.7 1.1 %copy-start = (f32[6,128,2,128]{3,2,1,0:T(2,128)S(1)}, f32[6,128,2,128]{3,2,1,0:T(2,128)}, u32[]{:S(2)}) copy-start(f32[6,128,2,128]{3,2,1,0:T(2,128)} %param.5) | copy-start | bytes 2359300
  1.8 1.1 %copy-start.1 = (f32[6,128,2,128]{3,2,1,0:T(2,128)S(1)}, f32[6,128,2,128]{3,2,1,0:T(2,128)}, u32[]{:S(2)}) copy-start(f32[6,128,2,128]{3,2,1,0:T(2,128)} %param.6) | copy-start | bytes 2359300
  2.9 1.0 %copy-start.2 = (bf16[6,128,2,128]{3,2,1,0:T(2,128)(2,1)S(1)}, bf16[6,128,2,128]{3,2,1,0:T(2,128)(2,1)}, u32[]{:S(2)}) copy-start(bf16[6,128,2,128]{3,2,1,0:T(2,128)(2,1)} %param.7) | copy-start | bytes 1179652
  3.9 0.9 %copy-start.3 = (f32[128,2,128]{2,1,0:T(2,128)S(1)}, f32[128,2,128]{2,1,0:T(2,128)}, u32[]{:S(2)}) copy-start(f32[128,2,128]{2,1,0:T(2,128)} %param.8) | copy-start | bytes 393220

commit v2 on v1

--- a/solution.py
+++ b/solution.py
@@ -14,7 +14,9 @@
 PAD = 8
 GROUP = 16
 MESH = pl.DeviceIdType.MESH
-HALO = jnp.float32
+HALO = jnp.bfloat16
+STEEP = 83.0
+CHUNKS = 8
 
 
 def total(parts):
@@ -22,6 +24,21 @@
     for part in parts[1:]:
         result = result + part
     return result
+
+
+def encode(values):
+    peak = jnp.abs(values[0])
+    for value in values[1:]:
+        peak = jnp.maximum(peak, jnp.abs(value))
+    peak = peak.astype(HALO)
+    factor = STEEP / jnp.maximum(peak.astype(jnp.float32), 1e-30)
+    return [jnp.exp(value * factor).astype(HALO) for value in values] + [peak]
+
+
+def decode(codes):
+    codes = [code.astype(jnp.float32) for code in codes]
+    factor = jnp.maximum(codes[-1], 1e-30) * (1.0 / STEEP)
+    return [jnp.log(code) * factor for code in codes[:-1]]
 
 
 def update(c, pm, pp, lo, hi, am, ap, prim, source, step):
@@ -59,10 +76,10 @@
 
 def kernel(
     n, comps, pitch, chunks,
-    counts, adj_in, src_in, st_in, ps_in, out,
-    adj, src, st, ps, prim, mid, fin,
+    counts_in, adj_in, src_in, st_in, ps_in, out,
+    counts, adj, src, st, ps, prim, mid,
     snd_dn, snd_up, rcv_lo, rcv_hi, gsend, gath, ghost, weight,
-    load_sem, store_sem, dn_send, dn_recv, up_send, up_recv, g_send, g_recv,
+    load_sem, dn_send, dn_recv, up_send, up_recv, g_send, g_recv,
 ):
     cells = 2 * pitch
     span = pitch // chunks
@@ -74,6 +91,7 @@
         pltpu.make_async_copy(st_in, st, load_sem.at[1]),
         pltpu.make_async_copy(src_in, src, load_sem.at[2]),
         pltpu.make_async_copy(ps_in, ps, load_sem.at[3]),
+        pltpu.make_async_copy(counts_in, counts, load_sem.at[4]),
     ]
     for load in loads:
         load.start()
@@ -86,6 +104,101 @@
 
     lane = lax.broadcasted_iota(jnp.int32, (1, LANES), 1)
 
+    def send_sums(sweep, sums):
+        message = jnp.zeros((1, LANES), f32)
+        for r in range(2):
+            for c in range(comps):
+                whole = jnp.sum(sums[r][c], axis=0, keepdims=True)
+                at = c + 8 * r
+                message = jnp.where(lane == at, pltpu.roll(whole, at, 1) if at else whole, message)
+                message = jnp.where(lane == at + 16, pltpu.roll(whole, at + 17, 1), message)
+        gsend[sweep] = message
+        gath[sweep, 0] = message
+
+    def sums_copy(sweep, k):
+        return pltpu.make_async_remote_copy(
+            src_ref=gsend.at[sweep],
+            dst_ref=gath.at[sweep, k],
+            send_sem=g_send.at[sweep, k],
+            recv_sem=g_recv.at[sweep, k],
+            device_id={"dom": lax.rem(me + k, n)},
+            device_id_type=MESH,
+        )
+
+    def down_copy(sweep, ch):
+        return pltpu.make_async_remote_copy(
+            src_ref=snd_dn.at[sweep, ch],
+            dst_ref=rcv_hi.at[sweep, ch],
+            send_sem=dn_send.at[sweep, ch],
+            recv_sem=dn_recv.at[sweep, ch],
+            device_id={"dom": jnp.maximum(me - 1, 0)},
+            device_id_type=MESH,
+        )
+
+    def up_copy(sweep, ch):
+        return pltpu.make_async_remote_copy(
+            src_ref=snd_up.at[sweep, ch],
+            dst_ref=rcv_lo.at[sweep, ch],
+            send_sem=up_send.at[sweep, ch],
+            recv_sem=up_recv.at[sweep, ch],
+            device_id={"dom": jnp.minimum(me + 1, n - 1)},
+            device_id_type=MESH,
+        )
+
+    def send_halo(sweep, ch):
+        @pl.when(me > 0)
+        def _():
+            down_copy(sweep, ch).start()
+
+        @pl.when(me < n - 1)
+        def _():
+            up_copy(sweep, ch).start()
+
+    def wrap(field):
+        field[:, PAD - 2 : PAD, :] = field[:, PAD + cells - 2 : PAD + cells, :]
+        field[:, PAD + cells : PAD + cells + 2, :] = field[:, PAD : PAD + 2, :]
+
+    zero_sums = tuple(jnp.zeros((8, LANES), f32) for _ in range(2 * comps))
+
+    def added(sums, r, values):
+        sums = list(sums)
+        for c in range(comps):
+            for part in range(GROUP // 8):
+                sums[r * comps + c] = sums[r * comps + c] + values[c][8 * part : 8 * part + 8]
+        return tuple(sums)
+
+    def split(sums):
+        return [sums[:comps], sums[comps:]]
+
+    loads[0].wait()
+
+    def first(ch, sums):
+        for part in range(span // GROUP):
+            at = pl.multiple_of(PAD + 2 * (ch * span + part * GROUP), 8)
+            for r in range(2):
+                values = [
+                    adj[c, pl.ds(at + r, GROUP, stride=2), :] for c in range(comps)
+                ]
+                target = (snd_dn, snd_up)[r]
+                for c, code in enumerate(encode(values)):
+                    target[0, ch, c, part * GROUP : (part + 1) * GROUP, :] = code
+                sums = added(sums, r, values)
+        return sums
+
+    sums = lax.fori_loop(0, chunks, first, zero_sums)
+    send_sums(0, split(sums))
+    pl.semaphore_wait(barrier, n - 1)
+    for k in range(1, n):
+        sums_copy(0, k).start()
+
+    def send_first(ch, carry):
+        send_halo(0, ch)
+        return carry
+
+    lax.fori_loop(0, chunks, send_first, 0)
+    wrap(adj)
+
+    loads[4].wait()
     starts, ends = [], []
     end = jnp.int32(0)
     for r in range(ROWS):
@@ -136,100 +249,6 @@
     below_ok = place > 0
     above_ok = place + 1 < my_count
 
-    def send_sums(sweep, sums):
-        message = jnp.zeros((1, LANES), f32)
-        for r in range(2):
-            for c in range(comps):
-                whole = jnp.sum(sums[r][c], axis=0, keepdims=True)
-                at = c + 8 * r
-                message = jnp.where(lane == at, pltpu.roll(whole, at, 1) if at else whole, message)
-                message = jnp.where(lane == at + 16, pltpu.roll(whole, at + 17, 1), message)
-        gsend[sweep] = message
-        gath[sweep, 0] = message
-
-    def sums_copy(sweep, k):
-        return pltpu.make_async_remote_copy(
-            src_ref=gsend.at[sweep],
-            dst_ref=gath.at[sweep, k],
-            send_sem=g_send.at[sweep, k],
-            recv_sem=g_recv.at[sweep, k],
-            device_id={"dom": lax.rem(me + k, n)},
-            device_id_type=MESH,
-        )
-
-    def down_copy(sweep, ch):
-        return pltpu.make_async_remote_copy(
-            src_ref=snd_dn.at[sweep, ch],
-            dst_ref=rcv_hi.at[sweep, ch],
-            send_sem=dn_send.at[sweep, ch],
-            recv_sem=dn_recv.at[sweep, ch],
-            device_id={"dom": jnp.maximum(me - 1, 0)},
-            device_id_type=MESH,
-        )
-
-    def up_copy(sweep, ch):
-        return pltpu.make_async_remote_copy(
-            src_ref=snd_up.at[sweep, ch],
-            dst_ref=rcv_lo.at[sweep, ch],
-            send_sem=up_send.at[sweep, ch],
-            recv_sem=up_recv.at[sweep, ch],
-            device_id={"dom": jnp.minimum(me + 1, n - 1)},
-            device_id_type=MESH,
-        )
-
-    def send_halo(sweep, ch):
-        @pl.when(me > 0)
-        def _():
-            down_copy(sweep, ch).start()
-
-        @pl.when(me < n - 1)
-        def _():
-            up_copy(sweep, ch).start()
-
-    def wrap(field):
-        field[:, PAD - 2 : PAD, :] = field[:, PAD + cells - 2 : PAD + cells, :]
-        field[:, PAD + cells : PAD + cells + 2, :] = field[:, PAD : PAD + 2, :]
-
-    zero_sums = tuple(jnp.zeros((8, LANES), f32) for _ in range(2 * comps))
-
-    def added(sums, r, values):
-        sums = list(sums)
-        for c in range(comps):
-            for part in range(GROUP // 8):
-                sums[r * comps + c] = sums[r * comps + c] + values[c][8 * part : 8 * part + 8]
-        return tuple(sums)
-
-    def split(sums):
-        return [sums[:comps], sums[comps:]]
-
-    loads[0].wait()
-
-    def first(ch, sums):
-        for part in range(span // GROUP):
-            at = pl.multiple_of(PAD + 2 * (ch * span + part * GROUP), 8)
-            for r in range(2):
-                values = [
-                    adj[c, pl.ds(at + r, GROUP, stride=2), :] for c in range(comps)
-                ]
-                target = (snd_dn, snd_up)[r]
-                for c in range(comps):
-                    target[0, ch, c, part * GROUP : (part + 1) * GROUP, :] = values[c].astype(HALO)
-                sums = added(sums, r, values)
-        return sums
-
-    sums = lax.fori_loop(0, chunks, first, zero_sums)
-    send_sums(0, split(sums))
-    pl.semaphore_wait(barrier, n - 1)
-    for k in range(1, n):
-        sums_copy(0, k).start()
-
-    def send_first(ch, carry):
-        send_halo(0, ch)
-        return carry
-
-    lax.fori_loop(0, chunks, send_first, 0)
-    wrap(adj)
-
     loads[1].wait()
 
     def primitive(j, carry):
@@ -248,9 +267,7 @@
     loads[2].wait()
     loads[3].wait()
 
-    for sweep in range(SWEEPS):
-        last = sweep == SWEEPS - 1
-        old = adj if sweep == 0 else mid
+    def make_ghosts(sweep):
         for k in range(1, n):
             sums_copy(sweep, k).wait_recv()
         gathered = gath[sweep][:, 0, :]
@@ -258,11 +275,17 @@
             mixed = jnp.sum(weight[i] * gathered, axis=0, keepdims=True)
             mixed = mixed + pltpu.roll(mixed, LANES - 8, 1)
             for c in range(comps):
-                ghost[sweep, i, c] = jnp.where(
+                ghost[i, c] = jnp.where(
                     lane == 0,
                     pltpu.roll(mixed, LANES - 16 - c, 1),
-                    pltpu.roll(mixed, LANES - 1 - c, 1),
+                    jnp.where(lane == LANES - 1, pltpu.roll(mixed, LANES - 1 - c, 1), 0.0),
                 )
+
+    for sweep in range(SWEEPS):
+        last = sweep == SWEEPS - 1
+        old = adj if sweep == 0 else mid
+        if not last:
+            make_ghosts(sweep)
 
         def advance(ch, sums, sweep=sweep, last=last, old=old):
             @pl.when(me < n - 1)
@@ -288,24 +311,20 @@
 
                     centre, before, after = near(0), near(-2), near(2)
                     if r == 0:
-                        below = [
-                            jnp.where(below_ok, rcv_lo[sweep, ch, c, piece, :].astype(f32), 0.0)
-                            for c in range(comps)
-                        ]
+                        codes = [rcv_lo[sweep, ch, c, piece, :] for c in range(comps + 1)]
+                        below = [jnp.where(below_ok, value, 0.0) for value in decode(codes)]
                         above = near(1)
                     else:
                         below = near(-1)
-                        above = [
-                            jnp.where(above_ok, rcv_hi[sweep, ch, c, piece, :].astype(f32), 0.0)
-                            for c in range(comps)
-                        ]
+                        codes = [rcv_hi[sweep, ch, c, piece, :] for c in range(comps + 1)]
+                        above = [jnp.where(above_ok, value, 0.0) for value in decode(codes)]
                     fore = [
-                        jnp.where(lane == 0, ghost[sweep, r, c], pltpu.roll(centre[c], 1, 1))
+                        jnp.where(lane == 0, 0.0 if last else ghost[r, c], pltpu.roll(centre[c], 1, 1))
                         for c in range(comps)
                     ]
                     aft = [
                         jnp.where(
-                            lane == LANES - 1, ghost[sweep, r, c],
+                            lane == LANES - 1, 0.0 if last else ghost[r, c],
                             pltpu.roll(centre[c], LANES - 1, 1),
                         )
                         for c in range(comps)
@@ -318,22 +337,17 @@
                     )
                     for c in range(comps):
                         if last:
-                            fin[c, pl.ds(at + r, GROUP, stride=2), :] = values[c]
+                            out[c, pl.ds(at + r, GROUP, stride=2), :] = values[c]
                         else:
                             mid[c, pl.ds(PAD + at + r, GROUP, stride=2), :] = values[c]
-                            target = (snd_dn, snd_up)[r]
-                            target[sweep + 1, ch, c, piece, :] = values[c].astype(HALO)
                     if not last:
+                        target = (snd_dn, snd_up)[r]
+                        for c, code in enumerate(encode(values)):
+                            target[sweep + 1, ch, c, piece, :] = code
                         sums = added(sums, r, values)
-            if last:
-                store(ch).start()
-            else:
+            if not last:
                 send_halo(sweep + 1, ch)
             return sums
-
-        def store(ch):
-            at = pl.ds(pl.multiple_of(2 * span * ch, 2 * span), 2 * span)
-            return pltpu.make_async_copy(fin.at[:, at, :], out.at[:, at, :], store_sem.at[ch])
 
         sums = lax.fori_loop(0, chunks, advance, () if last else zero_sums)
         if not last:
@@ -342,6 +356,36 @@
                 sums_copy(sweep + 1, k).start()
             wrap(mid)
 
+    make_ghosts(SWEEPS - 1)
+    odd = lax.broadcasted_iota(jnp.int32, (8, LANES), 0) % 2 == 1
+    around = [jnp.where(odd, ghost[1, c], ghost[0, c]) for c in range(comps)]
+    cross = [jnp.where(lane == 0, value, -value) for value in around]
+
+    def correct(j, carry):
+        for part in range(2):
+            at = pl.ds(pl.multiple_of(j * 16, 16) + 8 * part, 8)
+            v = [prim[k, at, :] for k in range(3)]
+            by_velocity = (
+                total([cross[1 + k] * v[k] for k in range(3)])
+                + cross[4] * prim[3, at, :] + cross[5] * prim[4, at, :]
+            )
+            energy = cross[4] * v[2]
+            by_pressure = cross[3] + energy
+            scaled = 0.4 * by_pressure
+            convected = [
+                prim[5, at, :] * by_pressure - v[2] * by_velocity,
+                cross[1] * v[2] - v[0] * scaled,
+                cross[2] * v[2] - v[1] * scaled,
+                cross[0] + cross[3] * v[2] - v[2] * scaled + by_velocity,
+                energy + scaled,
+                cross[5] * v[2],
+            ]
+            for c in range(comps):
+                out[c, at, :] = out[c, at, :] - ps[at, :] * (0.5 * convected[c] - around[c])
+        return carry
+
+    lax.fori_loop(0, cells // 16, correct, 0)
+
     def finish(ch, carry):
         for sweep in range(SWEEPS):
             @pl.when(me > 0)
@@ -351,7 +395,6 @@
             @pl.when(me < n - 1)
             def _():
                 up_copy(sweep, ch).wait_send()
-        store(ch).wait()
         return carry
 
     lax.fori_loop(0, chunks, finish, 0)
@@ -366,33 +409,32 @@
     span = pitch // chunks
     flat = (comps, cells, lanes)
     f32 = jnp.float32
-    hbm = pl.BlockSpec(memory_space=pl.ANY)
+    hbm = pl.BlockSpec(memory_space=pltpu.HBM)
     dma = pltpu.SemaphoreType.DMA
     padded = (comps, cells + 2 * PAD, lanes)
-    halo = (SWEEPS, chunks, comps, span, lanes)
+    halo = (SWEEPS, chunks, comps + 1, span, lanes)
     result = pl.pallas_call(
         functools.partial(kernel, n, comps, pitch, chunks),
-        out_shape=jax.ShapeDtypeStruct(flat, f32),
-        in_specs=[pl.BlockSpec(memory_space=pltpu.SMEM), hbm, hbm, hbm, hbm],
-        out_specs=hbm,
+        out_shape=pltpu.VMEM(flat, f32),
+        in_specs=[hbm] * 5,
+        out_specs=pl.BlockSpec(memory_space=pltpu.VMEM),
         scratch_shapes=[
+            pltpu.SMEM((ROWS,), jnp.int32),
             pltpu.VMEM(padded, f32),
             pltpu.VMEM(flat, f32),
             pltpu.VMEM(flat, jnp.bfloat16),
             pltpu.VMEM((cells, lanes), f32),
             pltpu.VMEM((6, cells, lanes), f32),
             pltpu.VMEM(padded, f32),
-            pltpu.VMEM(flat, f32),
             pltpu.VMEM(halo, HALO),
             pltpu.VMEM(halo, HALO),
             pltpu.VMEM(halo, HALO),
             pltpu.VMEM(halo, HALO),
             pltpu.VMEM((SWEEPS, 1, lanes), f32),
             pltpu.VMEM((SWEEPS, n, 1, lanes), f32),
-            pltpu.VMEM((SWEEPS, 2, comps, 1, lanes), f32),
+            pltpu.VMEM((2, comps, 1, lanes), f32),
             pltpu.VMEM((2, n, lanes), f32),
-            dma((4,)),
-            dma((chunks,)),
+            dma((5,)),
             dma((SWEEPS, chunks)),
             dma((SWEEPS, chunks)),
             dma((SWEEPS, chunks)),
@@ -401,7 +443,7 @@
             dma((SWEEPS, n)),
         ],
         compiler_params=pltpu.CompilerParams(
-            collective_id=0, has_side_effects=True, vmem_limit_bytes=32 * 1024 * 1024
+            collective_id=0, has_side_effects=True, vmem_limit_bytes=60 * 1024 * 1024
         ),
     )(
         row_counts,
@@ -415,7 +457,7 @@
 
 def solution(mesh):
     return jax.shard_map(
-        functools.partial(on_device, mesh.shape["dom"], 8),
+        functools.partial(on_device, mesh.shape["dom"], CHUNKS),
         mesh=mesh,
         in_specs=(
             P(None, None, ("groups", "dom"), None),

time: 34 us -> 21.4 us (0.63)
  Pallas kernels: 28 us -> 20.3 us
  local copies, waits for them, and re-layouts: 5.7 us -> 0.88 us
    pallas_call x1, Pallas kernels: 28 us -> 20.3 us  [on_device(): pl.pallas_call(functools.partial(kernel, n, comps, pitch, chunks), out_sh...]
    unnamed x11 -> x1, local copies, waits for them, and re-layouts: 5.7 us -> 0.88 us
where the time goes in v2:
time: 21.4 us; the launch traced here: 21.2 us
  Pallas kernels  20.3 us (95%)
  local copies, waits for them, and re-layouts  0.88 us (4%)
    pallas_call x1, Pallas kernels, on_device(): pl.pallas_call(functools.partial(kernel, n, comps, pitch, chunks), out_sh...  20.3 us
    unnamed x1, local copies, waits for them, and re-layouts  0.88 us

profile of v2, /device:TPU:0, one launch (start us, length us, event | category | flops | bytes accessed | tf_op | source)
XLA Modules:
  0.0 21.2 jit_solution(7337721154369102687)
XLA Ops:
  0.0 20.3 %shard_map.55 = f32[6,256,128]{2,1,0:T(8,128)S(1)} custom-call(s32[6]{0:T(128)} %counts_in.1, f32[6,256,128]{2,1,0:T(8,128)} %bitcast.6, f32[6,256,128]{2,1,0:T(8,128)} %bitcast.7, bf16[6,256,128]{2,1,0:T(8,128)(2,1)} %bitcast.8, f32[256,128]{1,0:T(8,128)} %bitcast.9), custom_call_target="tpu_custom_call" | custom-call | tf_op jit(solution)/shard_map/pallas_call | solution.py:416
  20.4 0.9 %copy.7 = f32[6,128,2,128]{3,2,1,0:T(2,128)} copy(f32[6,128,2,128]{3,2,1,0:T(2,128)S(1)} %bitcast.5) | data formatting | bytes 1572864

commit v3 on v2

--- a/solution.py
+++ b/solution.py
@@ -16,7 +16,7 @@
 MESH = pl.DeviceIdType.MESH
 HALO = jnp.bfloat16
 STEEP = 83.0
-CHUNKS = 8
+CHUNKS = 4
 
 
 def total(parts):
@@ -170,6 +170,16 @@
     def split(sums):
         return [sums[:comps], sums[comps:]]
 
+    def put_halo(sweep, ch, field):
+        at = pl.multiple_of(PAD + 2 * ch * span, 8)
+        for r, target in ((0, snd_dn), (1, snd_up)):
+            codes = encode([
+                field[c, pl.ds(at + r + 2 * GROUP * part, GROUP, stride=2), :]
+                for part in range(span // GROUP) for c in range(comps)
+            ])
+            for k, code in enumerate(codes):
+                target[sweep, ch, k] = code
+
     loads[0].wait()
 
     def first(ch, sums):
@@ -179,15 +189,14 @@
                 values = [
                     adj[c, pl.ds(at + r, GROUP, stride=2), :] for c in range(comps)
                 ]
-                target = (snd_dn, snd_up)[r]
-                for c, code in enumerate(encode(values)):
-                    target[0, ch, c, part * GROUP : (part + 1) * GROUP, :] = code
                 sums = added(sums, r, values)
+        put_halo(0, ch, adj)
         return sums
 
     sums = lax.fori_loop(0, chunks, first, zero_sums)
     send_sums(0, split(sums))
     pl.semaphore_wait(barrier, n - 1)
+    send_halo(0, 0)
     for k in range(1, n):
         sums_copy(0, k).start()
 
@@ -195,7 +204,7 @@
         send_halo(0, ch)
         return carry
 
-    lax.fori_loop(0, chunks, send_first, 0)
+    lax.fori_loop(1, chunks, send_first, 0)
     wrap(adj)
 
     loads[4].wait()
@@ -287,7 +296,7 @@
         if not last:
             make_ghosts(sweep)
 
-        def advance(ch, sums, sweep=sweep, last=last, old=old):
+        def advance(ch, sums, sweep=sweep, last=last, old=old, early=last):
             @pl.when(me < n - 1)
             def _():
                 down_copy(sweep, ch).wait_recv()
@@ -298,7 +307,11 @@
 
             for part in range(span // GROUP):
                 at = pl.multiple_of(2 * (ch * span + part * GROUP), 2 * GROUP)
-                piece = slice(part * GROUP, (part + 1) * GROUP)
+
+                def got(ref, part=part):
+                    kept = [ref[sweep, ch, part * comps + c] for c in range(comps)]
+                    return kept + [ref[sweep, ch, span // GROUP * comps]]
+
                 for r in range(2):
                     def near(offset):
                         return [
@@ -311,20 +324,20 @@
 
                     centre, before, after = near(0), near(-2), near(2)
                     if r == 0:
-                        codes = [rcv_lo[sweep, ch, c, piece, :] for c in range(comps + 1)]
+                        codes = got(rcv_lo)
                         below = [jnp.where(below_ok, value, 0.0) for value in decode(codes)]
                         above = near(1)
                     else:
                         below = near(-1)
-                        codes = [rcv_hi[sweep, ch, c, piece, :] for c in range(comps + 1)]
+                        codes = got(rcv_hi)
                         above = [jnp.where(above_ok, value, 0.0) for value in decode(codes)]
                     fore = [
-                        jnp.where(lane == 0, 0.0 if last else ghost[r, c], pltpu.roll(centre[c], 1, 1))
+                        jnp.where(lane == 0, 0.0 if early else ghost[r, c], pltpu.roll(centre[c], 1, 1))
                         for c in range(comps)
                     ]
                     aft = [
                         jnp.where(
-                            lane == LANES - 1, 0.0 if last else ghost[r, c],
+                            lane == LANES - 1, 0.0 if early else ghost[r, c],
                             pltpu.roll(centre[c], LANES - 1, 1),
                         )
                         for c in range(comps)
@@ -341,20 +354,20 @@
                         else:
                             mid[c, pl.ds(PAD + at + r, GROUP, stride=2), :] = values[c]
                     if not last:
-                        target = (snd_dn, snd_up)[r]
-                        for c, code in enumerate(encode(values)):
-                            target[sweep + 1, ch, c, piece, :] = code
                         sums = added(sums, r, values)
             if not last:
+                put_halo(sweep + 1, ch, mid)
                 send_halo(sweep + 1, ch)
             return sums
 
-        sums = lax.fori_loop(0, chunks, advance, () if last else zero_sums)
         if not last:
+            sums = lax.fori_loop(0, chunks, advance, zero_sums)
             send_sums(sweep + 1, split(sums))
             for k in range(1, n):
                 sums_copy(sweep + 1, k).start()
             wrap(mid)
+        else:
+            lax.fori_loop(0, chunks - 1, advance, ())
 
     make_ghosts(SWEEPS - 1)
     odd = lax.broadcasted_iota(jnp.int32, (8, LANES), 0) % 2 == 1
@@ -384,7 +397,8 @@
                 out[c, at, :] = out[c, at, :] - ps[at, :] * (0.5 * convected[c] - around[c])
         return carry
 
-    lax.fori_loop(0, cells // 16, correct, 0)
+    lax.fori_loop(0, (cells - 2 * span) // 16, correct, 0)
+    advance(chunks - 1, (), early=False)
 
     def finish(ch, carry):
         for sweep in range(SWEEPS):
@@ -412,7 +426,7 @@
     hbm = pl.BlockSpec(memory_space=pltpu.HBM)
     dma = pltpu.SemaphoreType.DMA
     padded = (comps, cells + 2 * PAD, lanes)
-    halo = (SWEEPS, chunks, comps + 1, span, lanes)
+    halo = (SWEEPS, chunks, span // GROUP * comps + 1, GROUP, lanes)
     result = pl.pallas_call(
         functools.partial(kernel, n, comps, pitch, chunks),
         out_shape=pltpu.VMEM(flat, f32),

time: 21.4 us -> 19.8 us (0.925)
  Pallas kernels: 20.3 us -> 18.8 us
    pallas_call x1, Pallas kernels: 20.3 us -> 18.8 us  [on_device(): pl.pallas_call(functools.partial(kernel, n, comps, pitch, chunks), out_sh...]
where the time goes in v3:
time: 19.8 us; the launch traced here: 19.7 us
  Pallas kernels  18.8 us (95%)
  local copies, waits for them, and re-layouts  0.88 us (4%)
    pallas_call x1, Pallas kernels, on_device(): pl.pallas_call(functools.partial(kernel, n, comps, pitch, chunks), out_sh...  18.8 us
    unnamed x1, local copies, waits for them, and re-layouts  0.88 us

profile of v3, /device:TPU:0, one launch (start us, length us, event | category | flops | bytes accessed | tf_op | source)
XLA Modules:
  0.0 19.7 jit_solution(8807809386119098584)
XLA Ops:
  0.0 18.8 %shard_map.55 = f32[6,256,128]{2,1,0:T(8,128)S(1)} custom-call(s32[6]{0:T(128)} %counts_in.1, f32[6,256,128]{2,1,0:T(8,128)} %bitcast.6, f32[6,256,128]{2,1,0:T(8,128)} %bitcast.7, bf16[6,256,128]{2,1,0:T(8,128)(2,1)} %bitcast.8, f32[256,128]{1,0:T(8,128)} %bitcast.9), custom_call_target="tpu_custom_call" | custom-call | tf_op jit(solution)/shard_map/pallas_call | solution.py:430
  18.8 0.9 %copy.7 = f32[6,128,2,128]{3,2,1,0:T(2,128)} copy(f32[6,128,2,128]{3,2,1,0:T(2,128)S(1)} %bitcast.5) | data formatting | bytes 1572864
